TPU v7x, 256 devices: a whole 4x4x8 slice. The times are simulated.
256 devices in a mesh: rows: 16 (over z, core), cols: 16 (over x, y).
Axes of the slice: x: 4, y: 4, z: 8, core: 2. Of those that a mesh axis runs over, the one named last changes fastest.
Arguments:
- source_points: float32 [32, 32768], P(None, ('rows', 'cols')), may hold values from -3.5 to 3.5
- target_points: float32 [32, 32768], P(None, ('cols', 'rows')), may hold values from -3.5 to 3.5
- target_init: float32 [32768], P('cols'), may hold values from -3 to 3
Outputs:
- source_potential: float32 [32768], P('rows')
- target_potential: float32 [32768], P('cols')
All inputs are finite; a program needn't handle non-finite values.
Results may differ from a plain program's by a relative error of at most 0.0003.
Values sent between devices are 32-bit elements; how exact they have to be, the bound alone decides.
A program may use at most 64 MiB of HBM per device.

v0:
```python
import math

import jax
import jax.numpy as jnp
from jax import lax
from jax.sharding import PartitionSpec as P

ITERS = 4


eps = 0.2


def cost_block(left, right, sq_left, sq_right):
    cross = lax.dot_general(
        left,
        right,
        (((0,), (0,)), ((), ())),
        precision=lax.Precision.HIGHEST,
        preferred_element_type=jnp.float32,
    )
    return sq_left[:, None] + sq_right[None, :] - 2.0 * cross


def split_blocks(points, width):
    return points.reshape(points.shape[0], points.shape[1] // width, width).transpose(1, 0, 2)


def row_partials(src_blocks, sq_blocks, targets, sq_targets, potential_g):

    def row_one_block(items):
        block, sq_block = items
        scores = (potential_g[None, :] - cost_block(block, targets, sq_block, sq_targets)) / eps
        peak = jnp.max(scores, axis=1)
        return (peak, jnp.sum(jnp.exp(scores - peak[:, None]), axis=1))

    peak, total = lax.map(row_one_block, (src_blocks, sq_blocks))
    return (peak.reshape(-1), total.reshape(-1))


def col_partials(sources, sq_sources, tgt_blocks, sq_blocks, potential_f):

    def col_one_block(items):
        block, sq_block = items
        scores = (potential_f[:, None] - cost_block(sources, block, sq_sources, sq_block)) / eps
        peak = jnp.max(scores, axis=0)
        return (peak, jnp.sum(jnp.exp(scores - peak[None, :]), axis=0))

    peak, total = lax.map(col_one_block, (tgt_blocks, sq_blocks))
    return (peak.reshape(-1), total.reshape(-1))


def finish_rows(peak, total, ntgt):
    whole_peak = lax.pmax(peak, "cols")
    whole_total = lax.psum(total * jnp.exp(peak - whole_peak), "cols")
    return eps * math.log(ntgt) - eps * (whole_peak + jnp.log(whole_total))


def finish_cols(peak, total, nsrc):
    whole_peak = lax.pmax(peak, "rows")
    whole_total = lax.psum(total * jnp.exp(peak - whole_peak), "rows")
    return eps * math.log(nsrc) - eps * (whole_peak + jnp.log(whole_total))


def body(source_points, target_points, target_init):
    sources = lax.all_gather(source_points, "cols", axis=1, tiled=True)
    targets = lax.all_gather(target_points, "rows", axis=1, tiled=True)
    nsrc = sources.shape[1] * lax.axis_size("rows")
    ntgt = targets.shape[1] * lax.axis_size("cols")
    sq_sources = jnp.sum(sources * sources, axis=0)
    sq_targets = jnp.sum(targets * targets, axis=0)
    width_src = min(128, sources.shape[1])
    width_tgt = min(128, targets.shape[1])
    src_blocks = split_blocks(sources, width_src)
    tgt_blocks = split_blocks(targets, width_tgt)
    sq_src_blocks = sq_sources.reshape(-1, width_src)
    sq_tgt_blocks = sq_targets.reshape(-1, width_tgt)
    potential_g = target_init
    potential_f = jnp.zeros((sources.shape[1],), jnp.float32)
    for step in range(ITERS):
        peak, total = row_partials(src_blocks, sq_src_blocks, targets, sq_targets, potential_g)
        potential_f = finish_rows(peak, total, ntgt)
        peak, total = col_partials(sources, sq_sources, tgt_blocks, sq_tgt_blocks, potential_f)
        potential_g = finish_cols(peak, total, nsrc)
    return (potential_f, potential_g)


def solution(mesh):
    in_specs = (P(None, ("rows", "cols")), P(None, ("cols", "rows")), P("cols"))
    out_specs = (P("rows"), P("cols"))
    return jax.shard_map(body, mesh=mesh, in_specs=in_specs, out_specs=out_specs, check_vma=False)
```

profile of v0, /device:TPU:1, one launch (start us, length us, event | category | flops | bytes accessed | tf_op | source)
XLA Modules:
  0.0 753.9 jit_solution(1587879278867175047)
XLA Ops:
  0.6 19.8 %all_gather.6 = f32[32,2048]{1,0:T(8,128)S(1)} all-gather(f32[32,128]{1,0:T(8,128)} %param.19), channel_id=1, replica_groups=mesh['rows'=16,'cols'=16] {'cols'}, dimensions={1}, use_global_device_ids=true | all-gather | bytes 278528 | tf_op jit(solution)/shard_map/all_gather | solution.py:66
  21.1 26.5 %all_gather.7 = f32[32,2048]{1,0:T(8,128)S(1)} all-gather(f32[32,128]{1,0:T(8,128)S(1)} %copy-done), channel_id=1, replica_groups=mesh['rows'=16,'cols'=16] {'rows'}, dimensions={1}, use_global_device_ids=true | all-gather | bytes 278528 | tf_op jit(solution)/shard_map/all_gather | solution.py:67
  48.4 26.9 %while.96 = (s32[]{:T(128)}, f32[16,128]{1,0:T(8,128)S(1)}, f32[16,128]{1,0:T(8,128)S(1)}, f32[2048]{0:T(1024)S(1)}, f32[16,128]{1,0:T(8,128)S(1)}, /*index=5*/f...) while((s32[]{:T(128)}, f32[16,128]{1,0:T(8,128)S(1)}, ...), condition=%wide.region_5.6_spmd, body=%wide.region_2.5_spmd.sunk | while | flops 102760192 | bytes 2397301 | solution.py:37
  50.1 1.3 fusion.86
  51.7 1.3 fusion.86
  53.4 1.3 fusion.86
  56.8 1.3 fusion.86
  58.5 1.3 fusion.86
  60.2 1.3 fusion.86
  63.5 1.3 fusion.86
  65.2 1.3 fusion.86
  66.9 1.3 fusion.86
  70.2 1.3 fusion.86
  71.9 1.3 fusion.86
  73.6 1.3 fusion.86
  75.3 31.7 %pmax.56 = f32[2048]{0:T(1024)S(1)} all-reduce(f32[2048]{0:T(1024)S(1)} %bitcast.240), channel_id=1, replica_groups=mesh['rows'=16,'cols'=16] {'cols'}, use_global_device_ids=true, to_apply=%region_6.7 | all-reduce | flops 2048 | bytes 16384 | tf_op jit(solution)/shard_map/pmax | solution.py:54
  106.9 29.3 %psum.56 = f32[2048]{0:T(1024)S(1)} all-reduce(f32[2048]{0:T(1024)S(1)} %bitcast_multiply_fusion.7), channel_id=1, replica_groups=mesh['rows'=16,'cols'=16] {'cols'}, use_global_device_ids=true, to_apply=%region_7.8 | all-reduce | flops 2048 | bytes 16384 | tf_op jit(solution)/shard_map/psum | solution.py:55
  136.5 26.9 %while.97 = (s32[]{:T(128)}, f32[16,128]{1,0:T(8,128)S(1)}, f32[16,128]{1,0:T(8,128)S(1)}, f32[2048]{0:T(1024)S(1)}, f32[2048]{0:T(1024)S(1)}, /*index=5*/f32[16...) while((s32[]{:T(128)}, f32[16,128]{1,0:T(8,128)S(1)}, ...), condition=%wide.region_11.12_spmd, body=%wide.region_8.11_spmd.sunk | while | flops 102760192 | bytes 2397301 | solution.py:49
  136.5 1.3 fusion.88
  163.4 37.4 %pmax.57 = f32[2048]{0:T(1024)S(1)} all-reduce(f32[2048]{0:T(1024)S(1)} %bitcast.241), channel_id=1, replica_groups=mesh['rows'=16,'cols'=16] {'rows'}, use_global_device_ids=true, to_apply=%region_12.13 | all-reduce | flops 2048 | bytes 16384 | tf_op jit(solution)/shard_map/pmax | solution.py:60
  200.8 24.1 %psum.57 = f32[2048]{0:T(1024)S(1)} all-reduce(f32[2048]{0:T(1024)S(1)} %bitcast_multiply_fusion.6), channel_id=1, replica_groups=mesh['rows'=16,'cols'=16] {'rows'}, use_global_device_ids=true, to_apply=%region_13.14 | all-reduce | flops 2048 | bytes 16384 | tf_op jit(solution)/shard_map/psum | solution.py:61
  224.9 27.0 %while.98 = (s32[]{:T(128)}, f32[16,128]{1,0:T(8,128)S(1)}, f32[16,128]{1,0:T(8,128)S(1)}, f32[2048]{0:T(1024)S(1)}, f32[16,128]{1,0:T(8,128)S(1)}, /*index=5*/f...) while((s32[]{:T(128)}, f32[16,128]{1,0:T(8,128)S(1)}, ...), condition=%wide.region_17.18_spmd, body=%wide.region_14.17_spmd.sunk | while | flops 102760192 | bytes 2397301 | solution.py:37
  225.0 1.3 fusion.90
  226.7 1.3 fusion.90
  230.0 1.3 fusion.90
  233.4 1.3 fusion.90
  236.8 1.3 fusion.90
  240.1 1.3 fusion.90
  243.5 1.3 fusion.90
  246.9 1.3 fusion.90
  250.2 1.3 fusion.90
  251.9 31.1 %pmax.58 = f32[2048]{0:T(1024)S(1)} all-reduce(f32[2048]{0:T(1024)S(1)} %bitcast.242), channel_id=1, replica_groups=mesh['rows'=16,'cols'=16] {'cols'}, use_global_device_ids=true, to_apply=%region_18.19 | all-reduce | flops 2048 | bytes 16384 | tf_op jit(solution)/shard_map/pmax | solution.py:54
  283.1 29.0 %psum.58 = f32[2048]{0:T(1024)S(1)} all-reduce(f32[2048]{0:T(1024)S(1)} %bitcast_multiply_fusion.5), channel_id=1, replica_groups=mesh['rows'=16,'cols'=16] {'cols'}, use_global_device_ids=true, to_apply=%region_19.20 | all-reduce | flops 2048 | bytes 16384 | tf_op jit(solution)/shard_map/psum | solution.py:55
  312.1 26.9 %while.99 = (s32[]{:T(128)}, f32[16,128]{1,0:T(8,128)S(1)}, f32[16,128]{1,0:T(8,128)S(1)}, f32[2048]{0:T(1024)S(1)}, f32[2048]{0:T(1024)S(1)}, /*index=5*/f32[16...) while((s32[]{:T(128)}, f32[16,128]{1,0:T(8,128)S(1)}, ...), condition=%wide.region_23.24_spmd, body=%wide.region_20.23_spmd.sunk | while | flops 102760192 | bytes 2397301 | solution.py:49
  339.0 37.9 %pmax.59 = f32[2048]{0:T(1024)S(1)} all-reduce(f32[2048]{0:T(1024)S(1)} %bitcast.243), channel_id=1, replica_groups=mesh['rows'=16,'cols'=16] {'rows'}, use_global_device_ids=true, to_apply=%region_24.25 | all-reduce | flops 2048 | bytes 16384 | tf_op jit(solution)/shard_map/pmax | solution.py:60
  377.0 24.1 %psum.59 = f32[2048]{0:T(1024)S(1)} all-reduce(f32[2048]{0:T(1024)S(1)} %bitcast_multiply_fusion.4), channel_id=1, replica_groups=mesh['rows'=16,'cols'=16] {'rows'}, use_global_device_ids=true, to_apply=%region_25.26 | all-reduce | flops 2048 | bytes 16384 | tf_op jit(solution)/shard_map/psum | solution.py:61
  401.0 27.0 %while.100 = (s32[]{:T(128)}, f32[16,128]{1,0:T(8,128)S(1)}, f32[16,128]{1,0:T(8,128)S(1)}, f32[2048]{0:T(1024)S(1)}, f32[16,128]{1,0:T(8,128)S(1)}, /*index=5*/...) while((s32[]{:T(128)}, f32[16,128]{1,0:T(8,128)S(1)}, ...), condition=%wide.region_29.30_spmd, body=%wide.region_26.29_spmd.sunk | while | flops 102760192 | bytes 2397301 | solution.py:37
  401.1 1.3 fusion.94
  402.8 1.3 fusion.94
  406.1 1.3 fusion.94
  409.5 1.3 fusion.94
  412.9 1.3 fusion.94
  416.2 1.3 fusion.94
  419.6 1.3 fusion.94
  423.0 1.3 fusion.94
  426.3 1.3 fusion.94
  428.0 31.1 %pmax.60 = f32[2048]{0:T(1024)S(1)} all-reduce(f32[2048]{0:T(1024)S(1)} %bitcast.244), channel_id=1, replica_groups=mesh['rows'=16,'cols'=16] {'cols'}, use_global_device_ids=true, to_apply=%region_30.31 | all-reduce | flops 2048 | bytes 16384 | tf_op jit(solution)/shard_map/pmax | solution.py:54
  459.1 29.0 %psum.60 = f32[2048]{0:T(1024)S(1)} all-reduce(f32[2048]{0:T(1024)S(1)} %bitcast_multiply_fusion.3), channel_id=1, replica_groups=mesh['rows'=16,'cols'=16] {'cols'}, use_global_device_ids=true, to_apply=%region_31.32 | all-reduce | flops 2048 | bytes 16384 | tf_op jit(solution)/shard_map/psum | solution.py:55
  488.2 26.9 %while.101 = (s32[]{:T(128)}, f32[16,128]{1,0:T(8,128)S(1)}, f32[16,128]{1,0:T(8,128)S(1)}, f32[2048]{0:T(1024)S(1)}, f32[2048]{0:T(1024)S(1)}, /*index=5*/f32[1...) while((s32[]{:T(128)}, f32[16,128]{1,0:T(8,128)S(1)}, ...), condition=%wide.region_35.36_spmd, body=%wide.region_32.35_spmd.sunk | while | flops 102760192 | bytes 2397301 | solution.py:49
  515.1 38.0 %pmax.61 = f32[2048]{0:T(1024)S(1)} all-reduce(f32[2048]{0:T(1024)S(1)} %bitcast.245), channel_id=1, replica_groups=mesh['rows'=16,'cols'=16] {'rows'}, use_global_device_ids=true, to_apply=%region_36.37 | all-reduce | flops 2048 | bytes 16384 | tf_op jit(solution)/shard_map/pmax | solution.py:60
  553.1 24.1 %psum.61 = f32[2048]{0:T(1024)S(1)} all-reduce(f32[2048]{0:T(1024)S(1)} %bitcast_multiply_fusion.2), channel_id=1, replica_groups=mesh['rows'=16,'cols'=16] {'rows'}, use_global_device_ids=true, to_apply=%region_37.38 | all-reduce | flops 2048 | bytes 16384 | tf_op jit(solution)/shard_map/psum | solution.py:61
  577.2 26.9 %while.102 = (s32[]{:T(128)}, f32[16,128]{1,0:T(8,128)S(1)}, f32[16,128]{1,0:T(8,128)S(1)}, f32[2048]{0:T(1024)S(1)}, f32[16,128]{1,0:T(8,128)S(1)}, /*index=5*/...) while((s32[]{:T(128)}, f32[16,128]{1,0:T(8,128)S(1)}, ...), condition=%wide.region_41.42_spmd, body=%wide.region_38.41_spmd.sunk | while | flops 102760192 | bytes 2397301 | solution.py:37
  577.2 1.3 fusion.98
  582.3 1.3 fusion.98
  585.6 1.3 fusion.98
  590.7 1.3 fusion.98
  594.0 1.3 fusion.98
  599.1 1.3 fusion.98
  602.5 1.3 fusion.98
  604.1 30.7 %pmax.62 = f32[2048]{0:T(1024)S(1)} all-reduce(f32[2048]{0:T(1024)S(1)} %bitcast.246), channel_id=1, replica_groups=mesh['rows'=16,'cols'=16] {'cols'}, use_global_device_ids=true, to_apply=%region_42.43 | all-reduce | flops 2048 | bytes 16384 | tf_op jit(solution)/shard_map/pmax | solution.py:54
  634.9 29.0 %psum.62 = f32[2048]{0:T(1024)S(1)} all-reduce(f32[2048]{0:T(1024)S(1)} %bitcast_multiply_fusion.1), channel_id=1, replica_groups=mesh['rows'=16,'cols'=16] {'cols'}, use_global_device_ids=true, to_apply=%region_43.44 | all-reduce | flops 2048 | bytes 16384 | tf_op jit(solution)/shard_map/psum | solution.py:55
  663.9 26.9 %while.103 = (s32[]{:T(128)}, f32[16,128]{1,0:T(8,128)S(1)}, f32[16,128]{1,0:T(8,128)S(1)}, f32[2048]{0:T(1024)S(1)}, f32[2048]{0:T(1024)S(1)}, /*index=5*/f32[1...) while((s32[]{:T(128)}, f32[16,128]{1,0:T(8,128)S(1)}, ...), condition=%wide.region_47.48_spmd, body=%wide.region_44.47_spmd.sunk | while | flops 102760192 | bytes 2397301 | solution.py:49
  690.9 38.3 %pmax.63 = f32[2048]{0:T(1024)S(1)} all-reduce(f32[2048]{0:T(1024)S(1)} %bitcast.239), channel_id=1, replica_groups=mesh['rows'=16,'cols'=16] {'rows'}, use_global_device_ids=true, to_apply=%region_48.49 | all-reduce | flops 2048 | bytes 16384 | tf_op jit(solution)/shard_map/pmax | solution.py:60
  729.2 24.1 %psum.63 = f32[2048]{0:T(1024)S(1)} all-reduce(f32[2048]{0:T(1024)S(1)} %bitcast_multiply_fusion), channel_id=1, replica_groups=mesh['rows'=16,'cols'=16] {'rows'}, use_global_device_ids=true, to_apply=%region_49.50 | all-reduce | flops 2048 | bytes 16384 | tf_op jit(solution)/shard_map/psum | solution.py:61
  (645 shorter events, 166.3 us)
Async XLA Ops:
  20.4 0.7 copy-start
  47.7 0.7 copy-start.2
  690.9 38.3 %copy-start.1 = (f32[2048]{0:T(1024)}, f32[2048]{0:T(1024)S(1)}, u32[]{:S(2)}) copy-start(f32[2048]{0:T(1024)S(1)} %get-tuple-element.1228) | copy-start | bytes 24580
where the time goes:
time: 755 us; the launch traced here: 754 us
  blocking collectives  535 us (71%)
  matrix products  163 us (22%)
  other arithmetic  40 us (5%)
  local copies, waits for them, and re-layouts  11.9 us (2%)
    dot_general x128, matrix products, cost_block(): lax.dot_general(left, right, (((0,), (0,)), ((), ())), precision=lax.Prec...  163 us
    pmax x4, blocking collectives, finish_cols(): whole_peak = lax.pmax(peak, 'rows')  152 us
    pmax x4, blocking collectives, finish_rows(): whole_peak = lax.pmax(peak, 'cols')  125 us
    psum x4, blocking collectives, finish_rows(): whole_total = lax.psum(total * jnp.exp(peak - whole_peak), 'cols')  116 us
    psum x4, blocking collectives, finish_cols(): whole_total = lax.psum(total * jnp.exp(peak - whole_peak), 'rows')  96.2 us
    all_gather x1, blocking collectives, body(): targets = lax.all_gather(target_points, 'rows', axis=1, tiled=True)  26.5 us
    all_gather x1, blocking collectives, body(): sources = lax.all_gather(source_points, 'cols', axis=1, tiled=True)  19.8 us
    reduce_sum x64, other arithmetic, row_one_block(): return (peak, jnp.sum(jnp.exp(scores - peak[:, None]), axis=1))  19.6 us

commit v1 on v0

v1 whole, which is shorter than its diff:
```python
import functools
import math

import jax
import jax.numpy as jnp
from jax import lax
from jax.experimental import pallas as pl
from jax.experimental.pallas import tpu as pltpu
from jax.sharding import PartitionSpec as P

ITERS = 4
EPS = 0.2
CHUNKS = 4
LANES = 128
ROWS_AT_ONCE = 64
DEPTH = 256
LOWEST = -1e30
TO_BITS = 1.0 / (EPS * math.log(2.0))
FROM_BITS = EPS * math.log(2.0)
MESH = pl.DeviceIdType.MESH


def ring_partners(me, size):
    steps = sorted(range(1, size), key=lambda k: -min(k // 2, (size - k) // 2))
    return [lax.rem(me + k, size) for k in steps]


def torus_partners(me, size):
    side = math.isqrt(size)
    x, y = lax.div(me, side), lax.rem(me, side)
    moves = [(a, b) for a in range(side) for b in range(side) if a + b > 0]
    moves.sort(key=lambda m: -(min(m[0], side - m[0]) + min(m[1], side - m[1])))
    return [lax.rem(x + a, side) * side + lax.rem(y + b, side) for a, b in moves]


def split3(x):
    hi = x.astype(jnp.bfloat16)
    rest = x - hi.astype(jnp.float32)
    mid = rest.astype(jnp.bfloat16)
    low = (rest - mid.astype(jnp.float32)).astype(jnp.bfloat16)
    return hi, mid, low


def send_to_all(src, dst, send_sem, recv_sem, axis, partners):
    for partner in partners:
        pltpu.make_async_remote_copy(
            src_ref=src,
            dst_ref=dst,
            send_sem=send_sem,
            recv_sem=recv_sem,
            device_id={axis: partner},
            device_id_type=MESH,
        ).start()


def wait_for_all(slots, sem):
    some = slots.at[pl.ds(0, slots.shape[0] - 1)]
    pltpu.make_async_copy(some, some, sem).wait()


def combine(parts):
    peak = jnp.max(parts, axis=0)
    return peak + jnp.log2(jnp.sum(jnp.exp2(parts - peak[None]), axis=0))


def spread(potential, wide, first):
    for q in range(potential.shape[0]):
        block = jnp.broadcast_to(potential[q : q + 1, :], (LANES, LANES))
        wide[pl.ds(pl.multiple_of(first + q * LANES, LANES), LANES), :] = block.T


def accumulate(scores, wide, first, count, lane_col, width, state):
    def step(r, state):
        rows = pl.ds(pl.multiple_of(first + r * ROWS_AT_ONCE, ROWS_AT_ONCE), ROWS_AT_ONCE)
        add = wide[rows, :]
        done = []
        for q in range(width):
            cols = pl.ds(pl.multiple_of((lane_col + q) * LANES, LANES), LANES)
            peak, total = state[q]
            z = (scores[rows, cols] + add).reshape(ROWS_AT_ONCE // 8, 8, LANES)
            top = jnp.maximum(peak, jnp.max(z, axis=0))
            total = total * jnp.exp2(peak - top) + jnp.sum(jnp.exp2(z - top[None]), axis=0)
            done.append((top, total))
        return tuple(done)

    steps = count // ROWS_AT_ONCE
    return lax.fori_loop(0, steps, step, state, unroll=min(8, steps))


def fresh(width):
    low = jnp.full((8, LANES), LOWEST, jnp.float32)
    return ((low, jnp.zeros((8, LANES), jnp.float32)),) * width


def finish(peak, total):
    top = jnp.max(peak, axis=0, keepdims=True)
    return top + jnp.log2(jnp.sum(total * jnp.exp2(peak - top), axis=0, keepdims=True))


def kernel(
    nr, nc, s_ref, t_ref, g_ref, f_out, g_out,
    s_all, t_all, s_cat, t_cat, s_rows, t_rows, w, wt, p_wide, q_wide, p_now, s_sq, t_sq, peaks, totals, p_parts, q_parts,
    pt_send, pt_recv, p_send, p_recv, q_send, q_recv,
):
    row, col = lax.axis_index("rows"), lax.axis_index("cols")
    in_rows = ring_partners(row, nr)
    in_cols = torus_partners(col, nc)
    n_src, n_tgt = nc * LANES, nr * LANES
    src_width, tgt_width = nc // CHUNKS, nr // CHUNKS
    bits_src = math.log2(n_src * nr)
    bits_tgt = math.log2(n_tgt * nc)

    barrier = pltpu.get_barrier_semaphore()
    for axis, partners in (("rows", in_rows), ("cols", in_cols)):
        for partner in partners:
            pl.semaphore_signal(barrier, inc=1, device_id={axis: partner}, device_id_type=MESH)
    pl.semaphore_wait(barrier, len(in_rows) + len(in_cols))

    send_to_all(t_ref, t_all.at[row], pt_send.at[0], pt_recv.at[0], "rows", in_rows)
    send_to_all(s_ref, s_all.at[col], pt_send.at[1], pt_recv.at[1], "cols", in_cols)
    t_all[row] = t_ref[...]
    s_all[col] = s_ref[...]
    empty = jnp.zeros((DEPTH - 6 * 32, LANES), jnp.bfloat16)

    def lay(points, scale, order, cat, turned, sq, q):
        x = points[q]
        sq[pl.ds(q, 1), :] = jnp.sum(x * x, axis=0, keepdims=True)
        pieces = split3(x * scale)
        block = jnp.concatenate([pieces[k] for k in order] + [empty], axis=0)
        at = pl.ds(pl.multiple_of(q * LANES, LANES), LANES)
        cat[:, at] = block
        turned[at, :] = block.T

    wait_for_all(s_all, pt_recv.at[1])

    @pl.loop(0, nc)
    def _(q):
        lay(s_all, 1.0, (0, 0, 1, 1, 0, 2), s_cat, s_rows, s_sq, q)

    wait_for_all(t_all, pt_recv.at[0])

    @pl.loop(0, nr)
    def _(q):
        lay(t_all, 2.0 * TO_BITS, (0, 1, 0, 1, 2, 0), t_cat, t_rows, t_sq, q)

    def products(left, right, out):
        @pl.loop(0, left.shape[0] // 256)
        def _(b):
            at = pl.ds(pl.multiple_of(b * 256, 256), 256)
            for c in range(right.shape[1] // 256):
                cols = pl.ds(c * 256, 256)
                out[at, cols] = jnp.dot(left[at, :], right[:, cols], preferred_element_type=jnp.float32)

    products(t_rows, s_cat, wt)
    products(s_rows, t_cat, w)
    spread((g_ref[...] - t_sq[...]) * TO_BITS, q_wide, 0)
    wait_for_all(t_all, pt_send.at[0])
    wait_for_all(s_all, pt_send.at[1])

    @pl.loop(0, ITERS)
    def _(it):
        @pl.loop(0, CHUNKS)
        def _(c):
            state = accumulate(wt, q_wide, 0, n_tgt, c * src_width, src_width, fresh(src_width))
            for q in range(src_width):
                p_parts[it, c, col, q : q + 1, :] = finish(*state[q])
            here = p_parts.at[it, c, col]
            send_to_all(here, here, p_send.at[it, c], p_recv.at[it, c], "cols", in_cols)

        @pl.loop(0, CHUNKS)
        def _(c):
            for q in range(tgt_width):
                peaks[c, q] = jnp.full((8, LANES), LOWEST, jnp.float32)
                totals[c, q] = jnp.zeros((8, LANES), jnp.float32)

        @pl.loop(0, CHUNKS)
        def _(c):
            wait_for_all(p_parts.at[it, c], p_send.at[it, c])
            wait_for_all(p_parts.at[it, c], p_recv.at[it, c])
            p = bits_tgt - combine(p_parts[it, c])
            p_now[c] = p
            depth = src_width * LANES
            spread(p, p_wide, c * depth)

            @pl.loop(0, CHUNKS)
            def _(d):
                state = tuple((peaks[d, q], totals[d, q]) for q in range(tgt_width))
                state = accumulate(w, p_wide, c * depth, depth, d * tgt_width, tgt_width, state)
                for q in range(tgt_width):
                    peaks[d, q], totals[d, q] = state[q]

                @pl.when(c == CHUNKS - 1)
                def _():
                    for q in range(tgt_width):
                        q_parts[it, d, row, q : q + 1, :] = finish(*state[q])
                    here = q_parts.at[it, d, row]
                    send_to_all(here, here, q_send.at[it, d], q_recv.at[it, d], "rows", in_rows)

        @pl.loop(0, CHUNKS)
        def _(d):
            wait_for_all(q_parts.at[it, d], q_send.at[it, d])
            wait_for_all(q_parts.at[it, d], q_recv.at[it, d])
            spread(bits_src - combine(q_parts[it, d]), q_wide, d * tgt_width * LANES)

    for c in range(CHUNKS):
        at = slice(c * src_width, (c + 1) * src_width)
        f_out[at, :] = s_sq[at, :] + FROM_BITS * p_now[c]
        at = slice(c * tgt_width, (c + 1) * tgt_width)
        g_out[at, :] = t_sq[at, :] + FROM_BITS * (bits_src - combine(q_parts[ITERS - 1, c]))


def body(source_points, target_points, target_init):
    nr, nc = lax.axis_size("rows"), lax.axis_size("cols")
    n_src, n_tgt = nc * LANES, nr * LANES
    f32, bf16 = jnp.float32, jnp.bfloat16
    src_width, tgt_width = nc // CHUNKS, nr // CHUNKS
    f, g = pl.pallas_call(
        functools.partial(kernel, nr, nc),
        out_shape=(jax.ShapeDtypeStruct((nc, LANES), f32), jax.ShapeDtypeStruct((nr, LANES), f32)),
        in_specs=[pl.BlockSpec(memory_space=pltpu.VMEM)] * 3,
        out_specs=[pl.BlockSpec(memory_space=pltpu.VMEM)] * 2,
        scratch_shapes=[
            pltpu.VMEM((nc,) + source_points.shape, f32),
            pltpu.VMEM((nr,) + target_points.shape, f32),
            pltpu.VMEM((DEPTH, n_src), bf16),
            pltpu.VMEM((DEPTH, n_tgt), bf16),
            pltpu.VMEM((n_src, DEPTH), bf16),
            pltpu.VMEM((n_tgt, DEPTH), bf16),
            pltpu.VMEM((n_src, n_tgt), f32),
            pltpu.VMEM((n_tgt, n_src), f32),
            pltpu.VMEM((n_src, LANES), f32),
            pltpu.VMEM((n_tgt, LANES), f32),
            pltpu.VMEM((CHUNKS, src_width, LANES), f32),
            pltpu.VMEM((nc, LANES), f32),
            pltpu.VMEM((nr, LANES), f32),
            pltpu.VMEM((CHUNKS, tgt_width, 8, LANES), f32),
            pltpu.VMEM((CHUNKS, tgt_width, 8, LANES), f32),
            pltpu.VMEM((ITERS, CHUNKS, nc, src_width, LANES), f32),
            pltpu.VMEM((ITERS, CHUNKS, nr, tgt_width, LANES), f32),
            pltpu.SemaphoreType.DMA((2,)),
            pltpu.SemaphoreType.DMA((2,)),
            pltpu.SemaphoreType.DMA((ITERS, CHUNKS)),
            pltpu.SemaphoreType.DMA((ITERS, CHUNKS)),
            pltpu.SemaphoreType.DMA((ITERS, CHUNKS)),
            pltpu.SemaphoreType.DMA((ITERS, CHUNKS)),
        ],
        compiler_params=pltpu.CompilerParams(
            collective_id=0, has_side_effects=True, vmem_limit_bytes=56 << 20
        ),
        name="sinkhorn",
    )(source_points, target_points, target_init.reshape(nr, LANES))
    return f.reshape(-1), g.reshape(-1)


def solution(mesh):
    in_specs = (P(None, ("rows", "cols")), P(None, ("cols", "rows")), P("cols"))
    out_specs = (P("rows"), P("cols"))
    return jax.shard_map(body, mesh=mesh, in_specs=in_specs, out_specs=out_specs, check_vma=False)
```

time: 755 us -> 96.5 us (0.13)
  blocking collectives: 535 us -> 0 us
  matrix products: 163 us -> 0 us
  Pallas kernels: 0 us -> 93.7 us
  other arithmetic: 40 us -> 0 us
  local copies, waits for them, and re-layouts: 11.9 us -> 1.9 us
    pmax x8 -> x0, blocking collectives: 276 us -> none  [the longest x4 152 us: finish_cols(): whole_peak = lax.pmax(peak, 'rows')]
    psum x8 -> x0, blocking collectives: 213 us -> none  [the longest x4 116 us: finish_rows(): whole_total = lax.psum(total * jnp.exp(peak - whole_peak), 'cols')]
    dot_general x128 -> x0, matrix products: 163 us -> none  [cost_block(): lax.dot_general(left, right, (((0,), (0,)), ((), ())), precision=lax.Prec...]
    pallas_call x0 -> x1, Pallas kernels: none -> 93.7 us  [body(): pl.pallas_call(functools.partial(kernel, nr, nc), out_shape=(jax.ShapeDty...]
    all_gather x2 -> x0, blocking collectives: 46.3 us -> none  [the longest x1 26.5 us: body(): targets = lax.all_gather(target_points, 'rows', axis=1, tiled=True)]
    reduce_sum x130 -> x0, other arithmetic: 39.3 us -> none  [the longest x64 19.6 us: row_one_block(): return (peak, jnp.sum(jnp.exp(scores - peak[:, None]), axis=1))]
    dynamic_update_slice x256 -> x0, local copies, waits for them, and re-layouts: 9.09 us -> none  [row_partials(): peak, total = lax.map(row_one_block, (src_blocks, sq_blocks))]
where the time goes in v1:
time: 96.5 us; the launch traced here: 96.3 us
  Pallas kernels  93.7 us (97%)
  local copies, waits for them, and re-layouts  1.9 us (2%)
    pallas_call x1, Pallas kernels, body(): pl.pallas_call(functools.partial(kernel, nr, nc), out_shape=(jax.ShapeDty...  93.7 us

profile of v1, /device:TPU:1, one launch (start us, length us, event | category | flops | bytes accessed | tf_op | source)
XLA Modules:
  0.0 96.3 jit_solution(6052844262940252477)
XLA Ops:
  0.6 93.7 %sinkhorn.1 = (f32[16,128]{1,0:T(8,128)}, f32[16,128]{1,0:T(8,128)}) custom-call(f32[32,128]{1,0:T(8,128)} %s_ref.1, f32[32,128]{1,0:T(8,128)} %t_ref.1, f32[16,128]{1,0:T(8,128)} %bitcast.3), custom_call_target="tpu_custom_call" | custom-call | tf_op jit(solution)/shard_map/sinkhorn/pallas_call | solution.py:217
  94.4 0.0 copy-start
  94.4 1.3 %copy.7 = f32[2048]{0:T(1024)} copy(f32[2048]{0:T(1024)} %bitcast.5) | data formatting | bytes 16384
  95.7 0.0 copy-done
  95.7 0.6 copy.8
Async XLA Ops:
  94.4 1.3 %copy-start = (f32[16,128]{1,0:T(8,128)S(1)}, f32[16,128]{1,0:T(8,128)}, u32[]{:S(2)}) copy-start(f32[16,128]{1,0:T(8,128)} %get-tuple-element.5) | copy-start | bytes 24580

commit v2 on v1

v2 whole, which is shorter than its diff:
```python
import functools
import math

import jax
import jax.numpy as jnp
from jax import lax
from jax.experimental import pallas as pl
from jax.experimental.pallas import tpu as pltpu
from jax.sharding import PartitionSpec as P

ITERS = 4
EPS = 0.2
SRC_CUTS = (8, 8)
TGT_CUTS = (8, 8)
LANES = 128
ROWS_AT_ONCE = 64
DEPTH = 256
LOWEST = -1e30
TO_BITS = 1.0 / (EPS * math.log(2.0))
FROM_BITS = EPS * math.log(2.0)
MESH = pl.DeviceIdType.MESH


def ring_partners(me, size):
    steps = sorted(range(1, size), key=lambda k: -min(k // 2, (size - k) // 2))
    return [lax.rem(me + k, size) for k in steps]


def torus_partners(me, size):
    side = math.isqrt(size)
    x, y = lax.div(me, side), lax.rem(me, side)
    moves = [(a, b) for a in range(side) for b in range(side) if a + b > 0]
    moves.sort(key=lambda m: -(min(m[0], side - m[0]) + min(m[1], side - m[1])))
    return [lax.rem(x + a, side) * side + lax.rem(y + b, side) for a, b in moves]


def split3(x):
    hi = x.astype(jnp.bfloat16)
    rest = x - hi.astype(jnp.float32)
    mid = rest.astype(jnp.bfloat16)
    low = (rest - mid.astype(jnp.float32)).astype(jnp.bfloat16)
    return hi, mid, low


def send_to_all(src, dst, send_sem, recv_sem, axis, partners):
    for partner in partners:
        pltpu.make_async_remote_copy(
            src_ref=src,
            dst_ref=dst,
            send_sem=send_sem,
            recv_sem=recv_sem,
            device_id={axis: partner},
            device_id_type=MESH,
        ).start()


def wait_for_all(slots, sem):
    some = slots.at[pl.ds(0, slots.shape[0] - 1)]
    pltpu.make_async_copy(some, some, sem).wait()


def combine(parts):
    peak = jnp.max(parts, axis=0)
    return peak + jnp.log2(jnp.sum(jnp.exp2(parts - peak[None]), axis=0))


def spread(potential, wide, first):
    for q in range(potential.shape[0]):
        block = jnp.broadcast_to(potential[q : q + 1, :], (LANES, LANES))
        wide[pl.ds(pl.multiple_of(first + q * LANES, LANES), LANES), :] = block.T


def accumulate(scores, wide, first, count, lane_col, width, state):
    def step(r, state):
        rows = pl.ds(pl.multiple_of(first + r * ROWS_AT_ONCE, ROWS_AT_ONCE), ROWS_AT_ONCE)
        add = wide[rows, :]
        done = []
        for q in range(width):
            cols = pl.ds((lane_col + q) * LANES, LANES)
            peak, total = state[q]
            z = (scores[rows, cols] + add).reshape(ROWS_AT_ONCE // 8, 8, LANES)
            top = jnp.maximum(peak, jnp.max(z, axis=0))
            total = total * jnp.exp2(peak - top) + jnp.sum(jnp.exp2(z - top[None]), axis=0)
            done.append((top, total))
        return tuple(done)

    steps = count // ROWS_AT_ONCE
    return lax.fori_loop(0, steps, step, state, unroll=min(max(8, 64 // width), steps))


def fresh(width):
    low = jnp.full((8, LANES), LOWEST, jnp.float32)
    return ((low, jnp.zeros((8, LANES), jnp.float32)),) * width


def finish(peak, total):
    top = jnp.max(peak, axis=0, keepdims=True)
    return top + jnp.log2(jnp.sum(total * jnp.exp2(peak - top), axis=0, keepdims=True))


def cut(cuts, blocks):
    unit = blocks // sum(cuts) if blocks >= sum(cuts) else 0
    widths = [c * unit for c in cuts] if unit else [blocks // 2, blocks // 2]
    return [(sum(widths[:k]), width) for k, width in enumerate(widths)]


def kernel(nr, nc, s_in, t_in, g_in, f_out, g_out, *scratch):
    scratch = list(scratch)
    s_all, t_all, s_cat, t_cat, s_rows, t_rows, w, wt, p_wide, q_wide, s_sq, t_sq, g_now, p_now = scratch[:14]
    local, s_sem, t_send, t_recv, p_sem, q_sem = scratch[14:20]
    src_chunks, tgt_chunks = cut(SRC_CUTS, nc), cut(TGT_CUTS, nr)
    p_parts = scratch[20 : 20 + len(src_chunks)]
    q_parts = scratch[20 + len(src_chunks) :]
    row, col = lax.axis_index("rows"), lax.axis_index("cols")
    in_rows = ring_partners(row, nr)
    in_cols = torus_partners(col, nc)
    n_src, n_tgt = nc * LANES, nr * LANES
    bits_src = math.log2(n_src * nr)
    bits_tgt = math.log2(n_tgt * nc)

    barrier = pltpu.get_barrier_semaphore()
    for axis, partners in (("rows", in_rows), ("cols", in_cols)):
        for partner in partners:
            pl.semaphore_signal(barrier, inc=1, device_id={axis: partner}, device_id_type=MESH)
    staged = [
        pltpu.make_async_copy(t_in, t_all.at[row], local.at[0]),
        pltpu.make_async_copy(s_in, s_all.at[col], local.at[1]),
        pltpu.make_async_copy(g_in, g_now, local.at[2]),
    ]
    for copy in staged:
        copy.start()
    for copy in staged:
        copy.wait()
    pl.semaphore_wait(barrier, len(in_rows) + len(in_cols))

    core = lax.rem(row, 2)
    sibling = row + 1 - 2 * core
    chips = nr // 2

    def far_row(step):
        return lax.rem(row + 2 * step, nr)

    def target_copy(shard, to, send_sem):
        return pltpu.make_async_remote_copy(
            src_ref=t_all.at[shard],
            dst_ref=t_all.at[shard],
            send_sem=send_sem,
            recv_sem=t_recv.at[shard],
            device_id={"rows": to},
            device_id_type=MESH,
        )

    by_distance = sorted(range(1, chips), key=lambda k: min(k, chips - k))
    for step in reversed(by_distance):
        target_copy(row, far_row(step), t_send.at[0]).start()
    here = s_all.at[col]
    send_to_all(here, here, s_sem.at[0], s_sem.at[1], "cols", in_cols)
    target_copy(row, sibling, t_send.at[1]).start()
    for step in by_distance:
        shard = far_row(step)
        target_copy(shard, sibling, t_send.at[1]).wait_recv()
        target_copy(shard, sibling, t_send.at[1]).start()
    empty = jnp.zeros((DEPTH - 6 * 32, LANES), jnp.bfloat16)

    def lay(points, scale, order, cat, turned, sq, q):
        x = points[q]
        sq[pl.ds(q, 1), :] = jnp.sum(x * x, axis=0, keepdims=True)
        pieces = split3(x * scale)
        block = jnp.concatenate([pieces[k] for k in order] + [empty], axis=0)
        at = pl.ds(pl.multiple_of(q * LANES, LANES), LANES)
        cat[:, at] = block
        turned[at, :] = block.T

    wait_for_all(s_all, s_sem.at[1])

    @pl.loop(0, nc)
    def _(q):
        lay(s_all, 1.0, (0, 0, 1, 1, 0, 2), s_cat, s_rows, s_sq, q)

    for step in [0] + by_distance:
        shard = far_row(step) + 1 - 2 * core
        target_copy(shard, sibling, t_send.at[1]).wait_recv()

    @pl.loop(0, nr)
    def _(q):
        lay(t_all, 2.0 * TO_BITS, (0, 1, 0, 1, 2, 0), t_cat, t_rows, t_sq, q)

    def products(left, right, out):
        tile = min(512, right.shape[1])

        @pl.loop(0, right.shape[1] // tile)
        def _(c):
            cols = pl.ds(pl.multiple_of(c * tile, tile), tile)
            out[:, cols] = jnp.dot(left[...], right[:, cols], preferred_element_type=jnp.float32)

    products(t_rows, s_cat, wt)
    spread((g_now[...] - t_sq[...]) * TO_BITS, q_wide, 0)

    @pl.loop(0, ITERS)
    def _(it):
        for c, (first, width) in enumerate(src_chunks):
            state = accumulate(wt, q_wide, 0, n_tgt, first, width, fresh(width))
            for q in range(width):
                p_parts[c][it, col, q : q + 1, :] = finish(*state[q])
            here = p_parts[c].at[it, col]
            send_to_all(here, here, p_sem.at[0, it, c], p_sem.at[1, it, c], "cols", in_cols)

        @pl.when(it == 0)
        def _():
            products(s_rows, t_cat, w)
            wait_for_all(s_all, s_sem.at[0])
            some = t_all.at[pl.ds(0, chips - 1)]
            pltpu.make_async_copy(some, some, t_send.at[0]).wait()
            some = t_all.at[pl.ds(0, chips)]
            pltpu.make_async_copy(some, some, t_send.at[1]).wait()

        whole = fresh(nr)
        for c, (first, width) in enumerate(src_chunks):
            wait_for_all(p_parts[c].at[it], p_sem.at[0, it, c])
            wait_for_all(p_parts[c].at[it], p_sem.at[1, it, c])
            p = bits_tgt - combine(p_parts[c][it])
            p_now[first : first + width, :] = p
            start, depth = first * LANES, width * LANES
            spread(p, p_wide, start)
            if c < len(src_chunks) - 1:
                whole = accumulate(w, p_wide, start, depth, 0, nr, whole)
                continue
            for d, (lane_col, cols) in enumerate(tgt_chunks):
                state = accumulate(w, p_wide, start, depth, lane_col, cols, whole[lane_col : lane_col + cols])
                for q in range(cols):
                    q_parts[d][it, row, q : q + 1, :] = finish(*state[q])
                here = q_parts[d].at[it, row]
                send_to_all(here, here, q_sem.at[0, it, d], q_sem.at[1, it, d], "rows", in_rows)

        for d, (first, width) in enumerate(tgt_chunks):
            wait_for_all(q_parts[d].at[it], q_sem.at[0, it, d])
            wait_for_all(q_parts[d].at[it], q_sem.at[1, it, d])
            q = bits_src - combine(q_parts[d][it])
            g_now[first : first + width, :] = q
            spread(q, q_wide, first * LANES)

    f_out[...] = s_sq[...] + FROM_BITS * p_now[...]
    g_out[...] = t_sq[...] + FROM_BITS * g_now[...]


def body(source_points, target_points, target_init):
    nr, nc = lax.axis_size("rows"), lax.axis_size("cols")
    n_src, n_tgt = nc * LANES, nr * LANES
    f32, bf16 = jnp.float32, jnp.bfloat16
    src_chunks, tgt_chunks = cut(SRC_CUTS, nc), cut(TGT_CUTS, nr)
    f, g = pl.pallas_call(
        functools.partial(kernel, nr, nc),
        out_shape=(jax.ShapeDtypeStruct((nc, LANES), f32), jax.ShapeDtypeStruct((nr, LANES), f32)),
        in_specs=[pl.BlockSpec(memory_space=pl.ANY)] * 3,
        out_specs=[pl.BlockSpec(memory_space=pltpu.VMEM)] * 2,
        scratch_shapes=[
            pltpu.VMEM((nc,) + source_points.shape, f32),
            pltpu.VMEM((nr,) + target_points.shape, f32),
            pltpu.VMEM((DEPTH, n_src), bf16),
            pltpu.VMEM((DEPTH, n_tgt), bf16),
            pltpu.VMEM((n_src, DEPTH), bf16),
            pltpu.VMEM((n_tgt, DEPTH), bf16),
            pltpu.VMEM((n_src, n_tgt), f32),
            pltpu.VMEM((n_tgt, n_src), f32),
            pltpu.VMEM((n_src, LANES), f32),
            pltpu.VMEM((n_tgt, LANES), f32),
            pltpu.VMEM((nc, LANES), f32),
            pltpu.VMEM((nr, LANES), f32),
            pltpu.VMEM((nr, LANES), f32),
            pltpu.VMEM((nc, LANES), f32),
            pltpu.SemaphoreType.DMA((3,)),
            pltpu.SemaphoreType.DMA((2,)),
            pltpu.SemaphoreType.DMA((2,)),
            pltpu.SemaphoreType.DMA((nr,)),
            pltpu.SemaphoreType.DMA((2, ITERS, len(src_chunks))),
            pltpu.SemaphoreType.DMA((2, ITERS, len(tgt_chunks))),
        ]
        + [pltpu.VMEM((ITERS, nc, width, LANES), f32) for _, width in src_chunks]
        + [pltpu.VMEM((ITERS, nr, width, LANES), f32) for _, width in tgt_chunks],
        compiler_params=pltpu.CompilerParams(
            collective_id=0, has_side_effects=True, vmem_limit_bytes=56 << 20
        ),
        name="sinkhorn",
    )(source_points, target_points, target_init.reshape(nr, LANES))
    return f.reshape(-1), g.reshape(-1)


def solution(mesh):
    in_specs = (P(None, ("rows", "cols")), P(None, ("cols", "rows")), P("cols"))
    out_specs = (P("rows"), P("cols"))
    return jax.shard_map(body, mesh=mesh, in_specs=in_specs, out_specs=out_specs, check_vma=False)
```

time: 96.5 us -> 85.2 us (0.88)
  Pallas kernels: 93.7 us -> 82.5 us
    pallas_call x1, Pallas kernels: 93.7 us -> 82.5 us  [body(): pl.pallas_call(functools.partial(kernel, nr, nc), out_shape=(jax.ShapeDty...]
where the time goes in v2:
time: 85.2 us; the launch traced here: 85 us
  Pallas kernels  82.5 us (97%)
  local copies, waits for them, and re-layouts  1.9 us (2%)
    pallas_call x1, Pallas kernels, body(): pl.pallas_call(functools.partial(kernel, nr, nc), out_shape=(jax.ShapeDty...  82.5 us
    unnamed x4, local copies, waits for them, and re-layouts  1.9 us

profile of v2, /device:TPU:1, one launch (start us, length us, event | category | flops | bytes accessed | tf_op | source)
XLA Modules:
  0.0 85.0 jit_solution(9108440722650167079)
XLA Ops:
  0.6 82.5 %sinkhorn.1 = (f32[16,128]{1,0:T(8,128)}, f32[16,128]{1,0:T(8,128)}) custom-call(f32[32,128]{1,0:T(8,128)} %s_in.1, f32[32,128]{1,0:T(8,128)} %t_in.1, f32[16,128]{1,0:T(8,128)} %bitcast.3), custom_call_target="tpu_custom_call" | custom-call | tf_op jit(solution)/shard_map/sinkhorn/pallas_call | solution.py:251
  83.1 0.0 copy-start
  83.1 1.3 %copy.7 = f32[2048]{0:T(1024)} copy(f32[2048]{0:T(1024)} %bitcast.5) | data formatting | bytes 16384
  84.4 0.0 copy-done
  84.4 0.6 copy.8
Async XLA Ops:
  83.1 1.3 %copy-start = (f32[16,128]{1,0:T(8,128)S(1)}, f32[16,128]{1,0:T(8,128)}, u32[]{:S(2)}) copy-start(f32[16,128]{1,0:T(8,128)} %get-tuple-element.5) | copy-start | bytes 24580

commit v3 on v2

--- a/solution.py
+++ b/solution.py
@@ -177,13 +177,24 @@
     def _(q):
         lay(s_all, 1.0, (0, 0, 1, 1, 0, 2), s_cat, s_rows, s_sq, q)
 
-    for step in [0] + by_distance:
-        shard = far_row(step) + 1 - 2 * core
+    def lay_target(shard):
+        lay(t_all, 2.0 * TO_BITS, (0, 1, 0, 1, 2, 0), t_cat, t_rows, t_sq, shard)
+        start = (g_now[pl.ds(shard, 1), :] - t_sq[pl.ds(shard, 1), :]) * TO_BITS
+        spread(start, q_wide, shard * LANES)
+
+    def nearest(k):
+        away = lax.div(k + 1, 2)
+        return lax.rem(row + 2 * (chips + (2 * lax.rem(k, 2) - 1) * away), nr)
+
+    @pl.loop(0, chips)
+    def _(k):
+        lay_target(nearest(k))
+
+    @pl.loop(0, chips)
+    def _(k):
+        shard = nearest(k) + 1 - 2 * core
         target_copy(shard, sibling, t_send.at[1]).wait_recv()
-
-    @pl.loop(0, nr)
-    def _(q):
-        lay(t_all, 2.0 * TO_BITS, (0, 1, 0, 1, 2, 0), t_cat, t_rows, t_sq, q)
+        lay_target(shard)
 
     def products(left, right, out):
         tile = min(512, right.shape[1])
@@ -194,12 +205,29 @@
             out[:, cols] = jnp.dot(left[...], right[:, cols], preferred_element_type=jnp.float32)
 
     products(t_rows, s_cat, wt)
-    spread((g_now[...] - t_sq[...]) * TO_BITS, q_wide, 0)
+
+    def take_target(it, d):
+        first, width = tgt_chunks[d]
+        wait_for_all(q_parts[d].at[it], q_sem.at[0, it, d])
+        wait_for_all(q_parts[d].at[it], q_sem.at[1, it, d])
+        q = bits_src - combine(q_parts[d][it])
+        g_now[first : first + width, :] = q
+        return q
 
     @pl.loop(0, ITERS)
     def _(it):
         for c, (first, width) in enumerate(src_chunks):
-            state = accumulate(wt, q_wide, 0, n_tgt, first, width, fresh(width))
+            state = fresh(width)
+            if c == 0:
+                for d, (lane_col, cols) in enumerate(tgt_chunks):
+
+                    @pl.when(it > 0)
+                    def _():
+                        spread(take_target(it - 1, d), q_wide, lane_col * LANES)
+
+                    state = accumulate(wt, q_wide, lane_col * LANES, cols * LANES, first, width, state)
+            else:
+                state = accumulate(wt, q_wide, 0, n_tgt, first, width, state)
             for q in range(width):
                 p_parts[c][it, col, q : q + 1, :] = finish(*state[q])
             here = p_parts[c].at[it, col]
@@ -232,15 +260,15 @@
                 here = q_parts[d].at[it, row]
                 send_to_all(here, here, q_sem.at[0, it, d], q_sem.at[1, it, d], "rows", in_rows)
 
-        for d, (first, width) in enumerate(tgt_chunks):
-            wait_for_all(q_parts[d].at[it], q_sem.at[0, it, d])
-            wait_for_all(q_parts[d].at[it], q_sem.at[1, it, d])
-            q = bits_src - combine(q_parts[d][it])
-            g_now[first : first + width, :] = q
-            spread(q, q_wide, first * LANES)
-
+    for d in range(len(tgt_chunks)):
+        take_target(ITERS - 1, d)
     f_out[...] = s_sq[...] + FROM_BITS * p_now[...]
     g_out[...] = t_sq[...] + FROM_BITS * g_now[...]
+
+
+def hand_over(f_ref, g_ref, f_out, g_out):
+    f_out[...] = f_ref[...]
+    g_out[...] = g_ref[...]
 
 
 def body(source_points, target_points, target_init):
@@ -282,6 +310,13 @@
         ),
         name="sinkhorn",
     )(source_points, target_points, target_init.reshape(nr, LANES))
+    f, g = pl.pallas_call(
+        hand_over,
+        out_shape=(jax.ShapeDtypeStruct((nc, LANES), f32), jax.ShapeDtypeStruct((nr, LANES), f32)),
+        in_specs=[pl.BlockSpec(memory_space=pltpu.VMEM)] * 2,
+        out_specs=[pl.BlockSpec(memory_space=pltpu.VMEM)] * 2,
+        name="hand_over",
+    )(f, g)
     return f.reshape(-1), g.reshape(-1)
 
 

time: 85.2 us -> 82.7 us (0.971)
  local copies, waits for them, and re-layouts: 1.9 us -> 0 us
    pallas_call x1, Pallas kernels: 82.5 us -> 80.4 us  [body(): pl.pallas_call(functools.partial(kernel, nr, nc), out_shape=(jax.ShapeDty...]
    unnamed x4 -> x0, local copies, waits for them, and re-layouts: 1.9 us -> none
    pallas_call x0 -> x1, Pallas kernels: none -> 1.32 us  [body(): pl.pallas_call(hand_over, out_shape=(jax.ShapeDtypeStruct((nc, LANES), f3...]
where the time goes in v3:
time: 82.7 us; the launch traced here: 82.4 us
  Pallas kernels  81.7 us (99%)
    pallas_call x1, Pallas kernels, body(): pl.pallas_call(functools.partial(kernel, nr, nc), out_shape=(jax.ShapeDty...  80.4 us

profile of v3, /device:TPU:1, one launch (start us, length us, event | category | flops | bytes accessed | tf_op | source)
XLA Modules:
  0.0 82.4 jit_solution(14633041259854570802)
XLA Ops:
  0.6 80.4 %sinkhorn.1 = (f32[16,128]{1,0:T(8,128)}, f32[16,128]{1,0:T(8,128)}) custom-call(f32[32,128]{1,0:T(8,128)} %s_in.1, f32[32,128]{1,0:T(8,128)} %t_in.1, f32[16,128]{1,0:T(8,128)} %bitcast.3), custom_call_target="tpu_custom_call" | custom-call | tf_op jit(solution)/shard_map/sinkhorn/pallas_call | solution.py:279
  81.1 1.3 %hand_over.1 = (f32[16,128]{1,0:T(8,128)}, f32[16,128]{1,0:T(8,128)}) custom-call(f32[16,128]{1,0:T(8,128)} %get-tuple-element.6.f_ref, f32[16,128]{1,0:T(8,128)} %get-tuple-element.7.g_ref), custom_call_target="tpu_custom_call" | custom-call | tf_op jit(solution)/shard_map/hand_over/pallas_call | solution.py:313

commit v4 on v3

--- a/solution.py
+++ b/solution.py
@@ -70,6 +70,12 @@
         wide[pl.ds(pl.multiple_of(first + q * LANES, LANES), LANES), :] = block.T
 
 
+def online(peak, total, z):
+    z = z.reshape(z.shape[0] // 8, 8, LANES)
+    top = jnp.maximum(peak, jnp.max(z, axis=0))
+    return top, total * jnp.exp2(peak - top) + jnp.sum(jnp.exp2(z - top[None]), axis=0)
+
+
 def accumulate(scores, wide, first, count, lane_col, width, state):
     def step(r, state):
         rows = pl.ds(pl.multiple_of(first + r * ROWS_AT_ONCE, ROWS_AT_ONCE), ROWS_AT_ONCE)
@@ -77,11 +83,7 @@
         done = []
         for q in range(width):
             cols = pl.ds((lane_col + q) * LANES, LANES)
-            peak, total = state[q]
-            z = (scores[rows, cols] + add).reshape(ROWS_AT_ONCE // 8, 8, LANES)
-            top = jnp.maximum(peak, jnp.max(z, axis=0))
-            total = total * jnp.exp2(peak - top) + jnp.sum(jnp.exp2(z - top[None]), axis=0)
-            done.append((top, total))
+            done.append(online(*state[q], scores[rows, cols] + add))
         return tuple(done)
 
     steps = count // ROWS_AT_ONCE
@@ -169,13 +171,14 @@
         block = jnp.concatenate([pieces[k] for k in order] + [empty], axis=0)
         at = pl.ds(pl.multiple_of(q * LANES, LANES), LANES)
         cat[:, at] = block
-        turned[at, :] = block.T
+        if turned is not None:
+            turned[at, :] = block.T
 
     wait_for_all(s_all, s_sem.at[1])
 
     @pl.loop(0, nc)
     def _(q):
-        lay(s_all, 1.0, (0, 0, 1, 1, 0, 2), s_cat, s_rows, s_sq, q)
+        lay(s_all, 1.0, (0, 0, 1, 1, 0, 2), s_cat, None, s_sq, q)
 
     def lay_target(shard):
         lay(t_all, 2.0 * TO_BITS, (0, 1, 0, 1, 2, 0), t_cat, t_rows, t_sq, shard)
@@ -204,7 +207,25 @@
             cols = pl.ds(pl.multiple_of(c * tile, tile), tile)
             out[:, cols] = jnp.dot(left[...], right[:, cols], preferred_element_type=jnp.float32)
 
-    products(t_rows, s_cat, wt)
+    for c, (first, width) in enumerate(src_chunks):
+
+        @pl.loop(0, width // 2)
+        def _(t):
+            cols = pl.ds(pl.multiple_of((first + 2 * t) * LANES, 2 * LANES), 2 * LANES)
+
+            def step(r, state):
+                rows = pl.ds(pl.multiple_of(r * LANES, LANES), LANES)
+                both = jnp.dot(t_rows[rows, :], s_cat[:, cols], preferred_element_type=jnp.float32)
+                add = q_wide[rows, :]
+                return tuple(online(*state[q], both[:, q * LANES : (q + 1) * LANES] + add) for q in range(2))
+
+            state = lax.fori_loop(0, nr, step, fresh(2), unroll=True)
+            for q in range(2):
+                p_parts[c][0, col, pl.ds(2 * t + q, 1), :] = finish(*state[q])
+
+        here = p_parts[c].at[0, col]
+        send_to_all(here, here, p_sem.at[0, 0, c], p_sem.at[1, 0, c], "cols", in_cols)
+
 
     def take_target(it, d):
         first, width = tgt_chunks[d]
@@ -214,17 +235,12 @@
         g_now[first : first + width, :] = q
         return q
 
-    @pl.loop(0, ITERS)
-    def _(it):
+    def row_pass(it):
         for c, (first, width) in enumerate(src_chunks):
             state = fresh(width)
             if c == 0:
                 for d, (lane_col, cols) in enumerate(tgt_chunks):
-
-                    @pl.when(it > 0)
-                    def _():
-                        spread(take_target(it - 1, d), q_wide, lane_col * LANES)
-
+                    spread(take_target(it - 1, d), q_wide, lane_col * LANES)
                     state = accumulate(wt, q_wide, lane_col * LANES, cols * LANES, first, width, state)
             else:
                 state = accumulate(wt, q_wide, 0, n_tgt, first, width, state)
@@ -233,8 +249,13 @@
             here = p_parts[c].at[it, col]
             send_to_all(here, here, p_sem.at[0, it, c], p_sem.at[1, it, c], "cols", in_cols)
 
+    @pl.loop(0, ITERS)
+    def _(it):
         @pl.when(it == 0)
         def _():
+            for q in range(nc):
+                at = pl.ds(q * LANES, LANES)
+                s_rows[at, :] = s_cat[:, at].T
             products(s_rows, t_cat, w)
             wait_for_all(s_all, s_sem.at[0])
             some = t_all.at[pl.ds(0, chips - 1)]
@@ -259,6 +280,14 @@
                     q_parts[d][it, row, q : q + 1, :] = finish(*state[q])
                 here = q_parts[d].at[it, row]
                 send_to_all(here, here, q_sem.at[0, it, d], q_sem.at[1, it, d], "rows", in_rows)
+
+        @pl.when(it == 0)
+        def _():
+            products(t_rows, s_cat, wt)
+
+        @pl.when(it < ITERS - 1)
+        def _():
+            row_pass(it + 1)
 
     for d in range(len(tgt_chunks)):
         take_target(ITERS - 1, d)

time: 82.7 us -> 81.3 us (0.983)
  Pallas kernels: 81.7 us -> 80.4 us
    pallas_call x1, Pallas kernels: 80.4 us -> 79.1 us  [body(): pl.pallas_call(functools.partial(kernel, nr, nc), out_shape=(jax.ShapeDty...]
where the time goes in v4:
time: 81.3 us; the launch traced here: 81 us
  Pallas kernels  80.4 us (99%)
    pallas_call x1, Pallas kernels, body(): pl.pallas_call(functools.partial(kernel, nr, nc), out_shape=(jax.ShapeDty...  79.1 us

profile of v4, /device:TPU:1, one launch (start us, length us, event | category | flops | bytes accessed | tf_op | source)
XLA Modules:
  0.0 81.0 jit_solution(17302555594134009247)
XLA Ops:
  0.6 79.1 %sinkhorn.1 = (f32[16,128]{1,0:T(8,128)}, f32[16,128]{1,0:T(8,128)}) custom-call(f32[32,128]{1,0:T(8,128)} %s_in.1, f32[32,128]{1,0:T(8,128)} %t_in.1, f32[16,128]{1,0:T(8,128)} %bitcast.3), custom_call_target="tpu_custom_call" | custom-call | tf_op jit(solution)/shard_map/sinkhorn/pallas_call | solution.py:308
  79.7 1.3 %hand_over.1 = (f32[16,128]{1,0:T(8,128)}, f32[16,128]{1,0:T(8,128)}) custom-call(f32[16,128]{1,0:T(8,128)} %get-tuple-element.6.f_ref, f32[16,128]{1,0:T(8,128)} %get-tuple-element.7.g_ref), custom_call_target="tpu_custom_call" | custom-call | tf_op jit(solution)/shard_map/hand_over/pallas_call | solution.py:342

commit v5 on v4

--- a/solution.py
+++ b/solution.py
@@ -176,7 +176,7 @@
 
     wait_for_all(s_all, s_sem.at[1])
 
-    @pl.loop(0, nc)
+    @pl.loop(0, nc, unroll=4)
     def _(q):
         lay(s_all, 1.0, (0, 0, 1, 1, 0, 2), s_cat, None, s_sq, q)
 
@@ -189,7 +189,7 @@
         away = lax.div(k + 1, 2)
         return lax.rem(row + 2 * (chips + (2 * lax.rem(k, 2) - 1) * away), nr)
 
-    @pl.loop(0, chips)
+    @pl.loop(0, chips, unroll=min(4, chips))
     def _(k):
         lay_target(nearest(k))
 

time: 81.3 us -> 81 us (level)
  no operation moved by 1% of the time
where the time goes in v5:
time: 81 us; the launch traced here: 80.7 us
  Pallas kernels  80.1 us (99%)
    pallas_call x1, Pallas kernels, body(): pl.pallas_call(functools.partial(kernel, nr, nc), out_shape=(jax.ShapeDty...  78.8 us

profile of v5, /device:TPU:1, one launch (start us, length us, event | category | flops | bytes accessed | tf_op | source)
XLA Modules:
  0.0 80.7 jit_solution(5875222648860006636)
XLA Ops:
  0.6 78.8 %sinkhorn.1 = (f32[16,128]{1,0:T(8,128)}, f32[16,128]{1,0:T(8,128)}) custom-call(f32[32,128]{1,0:T(8,128)} %s_in.1, f32[32,128]{1,0:T(8,128)} %t_in.1, f32[16,128]{1,0:T(8,128)} %bitcast.3), custom_call_target="tpu_custom_call" | custom-call | tf_op jit(solution)/shard_map/sinkhorn/pallas_call | solution.py:308
  79.4 1.3 %hand_over.1 = (f32[16,128]{1,0:T(8,128)}, f32[16,128]{1,0:T(8,128)}) custom-call(f32[16,128]{1,0:T(8,128)} %get-tuple-element.6.f_ref, f32[16,128]{1,0:T(8,128)} %get-tuple-element.7.g_ref), custom_call_target="tpu_custom_call" | custom-call | tf_op jit(solution)/shard_map/hand_over/pallas_call | solution.py:342

commit v6 on v5

--- a/solution.py
+++ b/solution.py
@@ -195,9 +195,11 @@
 
     @pl.loop(0, chips)
     def _(k):
-        shard = nearest(k) + 1 - 2 * core
-        target_copy(shard, sibling, t_send.at[1]).wait_recv()
-        lay_target(shard)
+        target_copy(nearest(k) + 1 - 2 * core, sibling, t_send.at[1]).wait_recv()
+
+    @pl.loop(0, chips, unroll=min(4, chips))
+    def _(k):
+        lay_target(nearest(k) + 1 - 2 * core)
 
     def products(left, right, out):
         tile = min(512, right.shape[1])

time: 81 us -> 81 us (level)
  no operation moved by 1% of the time
where the time goes in v6:
time: 81 us; the launch traced here: 80.7 us
  Pallas kernels  80.1 us (99%)
    pallas_call x1, Pallas kernels, body(): pl.pallas_call(functools.partial(kernel, nr, nc), out_shape=(jax.ShapeDty...  78.8 us

profile of v6, /device:TPU:1, one launch (start us, length us, event | category | flops | bytes accessed | tf_op | source)
XLA Modules:
  0.0 80.7 jit_solution(5251915737942818173)
XLA Ops:
  0.6 78.8 %sinkhorn.1 = (f32[16,128]{1,0:T(8,128)}, f32[16,128]{1,0:T(8,128)}) custom-call(f32[32,128]{1,0:T(8,128)} %s_in.1, f32[32,128]{1,0:T(8,128)} %t_in.1, f32[16,128]{1,0:T(8,128)} %bitcast.3), custom_call_target="tpu_custom_call" | custom-call | tf_op jit(solution)/shard_map/sinkhorn/pallas_call | solution.py:310
  79.4 1.3 %hand_over.1 = (f32[16,128]{1,0:T(8,128)}, f32[16,128]{1,0:T(8,128)}) custom-call(f32[16,128]{1,0:T(8,128)} %get-tuple-element.6.f_ref, f32[16,128]{1,0:T(8,128)} %get-tuple-element.7.g_ref), custom_call_target="tpu_custom_call" | custom-call | tf_op jit(solution)/shard_map/hand_over/pallas_call | solution.py:344
